TPU v7x, 256 devices: a whole 4x4x8 slice. The times are simulated.
256 devices in a mesh: dp: 64 (over z, x, core), tensor: 4 (over y).
Axes of the slice: x: 4, y: 4, z: 8, core: 2. Of those that a mesh axis runs over, the one named last changes fastest.
Arguments:
- grad_blocks: float32 [128, 512, 512], P('tensor', 'dp'), may hold values from -420 to 420
- owner_map: int32 [4, 32], replicated, may hold values from 0 to 63, as said below
- left_state: float32 [4, 64, 2, 512, 512], P('tensor', 'dp'), may hold values from -1 to 5, as said below
- right_state: float32 [4, 64, 2, 512, 512], P('tensor', 'dp'), may hold values from -1 to 5, as said below
Outputs:
- step_blocks: float32 [128, 512, 512], P('tensor', 'dp')
- new_left: float32 [4, 64, 2, 512, 512], P('tensor', 'dp')
- new_right: float32 [4, 64, 2, 512, 512], P('tensor', 'dp')
Inputs may be any that keep to these rules, and one draw needn't show every extreme that they name: `owner_map`: within one tensor index every dp index owns at most 2 blocks, and one owns exactly 2. `left_state`: every block is symmetric positive definite. `right_state`: every block is symmetric positive definite.
All inputs are finite; a program needn't handle non-finite values.
Results may differ from a plain program's by a relative error of at most 0.013.
Values sent between devices are 32-bit elements; how exact they have to be, the bound alone decides.
A program may use at most 64 MiB of HBM per device.

v0:
```python
import jax
import jax.numpy as jnp
from jax import lax
from jax.sharding import PartitionSpec as P

ITERS = 2


def product(left_op, right_op):
    return jnp.dot(
        left_op.astype(jnp.bfloat16),
        right_op.astype(jnp.bfloat16),
        preferred_element_type=jnp.float32,
    )


def inverse_root(factor):
    identity = jnp.eye(factor.shape[0], dtype=jnp.float32)
    scaling = 2.5 / jnp.sqrt(jnp.sum(factor * factor) + 1e-06)
    root_est = jnp.sqrt(jnp.sqrt(scaling)) * identity
    matrix = scaling * factor
    for sweep in range(ITERS):
        stepper = 1.25 * identity - 0.25 * matrix
        root_est = product(root_est, stepper)
        square = product(stepper, stepper)
        fourth = product(square, square)
        matrix = product(fourth, matrix)
    return root_est


def update_slot(items):
    clipped, left_old, right_old = items
    block_order = clipped.shape[0]
    gram_left = lax.dot_general(
        clipped, clipped, (((1,), (1,)), ((), ())), precision=lax.Precision.HIGHEST
    )
    gram_right = lax.dot_general(
        clipped, clipped, (((0,), (0,)), ((), ())), precision=lax.Precision.HIGHEST
    )
    left_new = 0.9 * left_old + 0.1 * gram_left / block_order
    right_new = 0.9 * right_old + 0.1 * gram_right / block_order
    left_root = inverse_root(left_new)
    right_root = inverse_root(right_new)
    middle = product(left_root, clipped).astype(jnp.bfloat16)
    direction = jnp.dot(middle, right_root.astype(jnp.bfloat16), preferred_element_type=jnp.float32)
    graft_ratio = jnp.sqrt(jnp.sum(clipped * clipped) + 1e-06) / jnp.sqrt(
        jnp.sum(direction * direction) + 1e-06
    )
    return (-graft_ratio * direction, left_new, right_new)


def local(grad_blocks, owner_map, left_state, right_state):
    block_count, rows_dev, block_order = grad_blocks.shape
    slot_count = left_state.shape[2]
    dp_size = lax.axis_size("dp")
    tensor_size = lax.axis_size("tensor")
    tensor_index = lax.axis_index("tensor")
    my_index = lax.axis_index("dp")
    owners = lax.dynamic_slice_in_dim(owner_map, tensor_index, 1, 0)[0]
    positions = jnp.arange(block_count)
    same_owner = owners[:, None] == owners[None, :]
    earlier = positions[:, None] < positions[None, :]
    slot_of = jnp.sum(jnp.where(same_owner & earlier, 1, 0), axis=0)
    target = owners * slot_count + slot_of
    selector = (jnp.arange(dp_size * slot_count)[:, None] == target[None, :]).astype(jnp.float32)
    packed = jnp.einsum("kj,jrb->krb", selector, grad_blocks, precision=lax.Precision.HIGHEST)
    packed = packed.reshape(dp_size, slot_count, rows_dev, block_order)
    arrived = lax.all_to_all(packed, "dp", split_axis=0, concat_axis=2, tiled=True)[0]
    entries = block_count * tensor_size * block_order * block_order
    squares = lax.psum(jnp.sum(arrived * arrived), ("dp", "tensor"))
    clip_factor = 1.0 / jnp.sqrt(squares / entries + 1e-06)
    owned = jnp.sum(jnp.where(owners == my_index, 1, 0))
    filled = (jnp.arange(slot_count) < owned).astype(jnp.float32)[:, None, None]
    step_slots, left_new, right_new = lax.map(
        update_slot, (clip_factor * arrived, left_state[0, 0], right_state[0, 0])
    )
    returned = lax.all_to_all(step_slots[None], "dp", split_axis=2, concat_axis=0, tiled=True)
    returned = returned.reshape(dp_size * slot_count, rows_dev, block_order)
    step_blocks = jnp.einsum("kj,krb->jrb", selector, returned, precision=lax.Precision.HIGHEST)
    return (step_blocks, (filled * left_new)[None, None], (filled * right_new)[None, None])


def solution(mesh):
    placed = (
        P("tensor", "dp", None),
        P(),
        P("tensor", "dp", None, None, None),
        P("tensor", "dp", None, None, None),
    )
    return jax.shard_map(
        local,
        mesh=mesh,
        in_specs=placed,
        out_specs=(
            P("tensor", "dp", None),
            P("tensor", "dp", None, None, None),
            P("tensor", "dp", None, None, None),
        ),
        check_vma=False,
    )
```

profile of v0, /device:TPU:1, one launch (start us, length us, event | category | flops | bytes accessed | tf_op | source)
XLA Modules:
  0.0 330.9 jit_solution(700596265658305211)
XLA Ops:
  2.8 2.5 fusion.32
  5.3 2.5 reshape.30
  7.8 2.6 copy.18
  10.4 13.0 %all-to-all-start = ((f32[64,2,8,512]{3,1,2,0:T(2,128)}), f32[64,2,8,512]{3,1,2,0:T(2,128)S(1)}, u32[]{:S(2)}, u32[]{:S(2)}) async-start(f32[64,2,8,512]{3,1,2,0:T(2,128)} %copy.18), calls=%async_computation | async-start | bytes 4194304 | tf_op jit(solution)/shard_map/all_to_all | solution.py:68
  23.4 49.7 %all-to-all-done = f32[64,2,8,512]{3,1,2,0:T(2,128)S(1)} async-done(((f32[64,2,8,512]{3,1,2,0:T(2,128)}), f32[64,2,8,512]{3,1,2,0:T(2,128)S(1)}, u32[]{:S(2)}, u32[]{:S(2)}) %all-to-all-start) | async-done | bytes 2097184 | tf_op jit(solution)/shard_map/all_to_all | solution.py:68
  73.1 2.8 multiply_reduce_fusion.4
  75.8 76.7 %psum.7 = f32[]{:T(128)} all-reduce(f32[]{:T(128)} %multiply_reduce_fusion.4), channel_id=1, replica_groups=mesh['dp'=64,'tensor'=4] {'dp','tensor'}, use_global_device_ids=true, to_apply=%region_2.3 | all-reduce | flops 1 | bytes 8 | tf_op jit(solution)/shard_map/psum | solution.py:70
  154.8 113.6 %while.17 = (s32[]{:T(128)}, f32[2,512,512]{2,0,1:T(2,128)}, f32[2,512,512]{2,1,0:T(8,128)}, f32[2,512,512]{2,1,0:T(8,128)}, f32[2,512,512]{2,0,1:T(2,128)}, /*i...) while((s32[]{:T(128)}, f32[2,512,512]{2,0,1:T(2,128)}, ...), condition=%wide.region_8.9_spmd, body=%wide.region_3.8_spmd.sunk | while | flops 6459752448 | bytes 38797676 | solution.py:74
  154.8 2.5 constant_dynamic-slice_fusion.3
  158.9 3.9 %multiply_reduce_fusion.10 = (f32[]{:T(128)}, f32[512,512]{1,0:T(8,128)S(1)}) fusion(f32[1,512,512]{2,0,1:T(1,128)S(1)} %constant_dynamic-slice_fusion.3, f32[2,512,512]{2,1,0:T(8,128)} %get-tuple-element.252, s32[]{:T(128)S(6)} %copy.63), kind=kOutput, calls=%fused_computation.32.clone.1 | convolution fusion | flops 1611923456 | bytes 3145736 | tf_op jit(solution)/shard_map/while/body/eval_jaxpr/dot_general | solution.py:34
  165.9 1.8 convolution_convert_fusion.16
  167.7 4.7 %multiply_reduce_fusion.9 = (f32[]{:T(128)}, f32[512,512]{1,0:T(8,128)}) fusion(f32[1,512,512]{2,0,1:T(1,128)S(1)} %constant_dynamic-slice_fusion.3, f32[2,512,512]{2,1,0:T(8,128)} %get-tuple-element.253, s32[]{:T(128)S(6)} %copy.63), kind=kOutput, calls=%fused_computation.30.clone.1 | convolution fusion | flops 1611923456 | bytes 3145736 | tf_op jit(solution)/shard_map/while/body/eval_jaxpr/dot_general | solution.py:37
  173.2 4.4 %convolution_convert_fusion.13 = bf16[512,512]{1,0:T(8,128)(2,1)} fusion(f32[512,512]{1,0:T(8,128)} %get-tuple-element.217, f32[]{:T(128)S(6)} %div.33), kind=kOutput, calls=%fused_computation.11.clone.1 | convolution fusion | flops 538968064 | bytes 1572868 | tf_op jit(solution)/shard_map/while/body/eval_jaxpr/dot_general | solution.py:10
  177.6 2.6 fusion.78
  180.3 2.9 convolution_convert_fusion.14
  183.2 3.4 %multiply_reduce_fusion.11 = (f32[]{:T(128)}, f32[512,512]{1,0:T(8,128)}) fusion(bf16[512,512]{1,0:T(8,128)(2,1)} %convolution_convert_fusion.14, bf16[512,512]{1,0:T(8,128)(2,1)S(1)} %convolution_convert_fusion.16, f32[1,512,512]{2,0,1:T(1,128)S(1)} %constant_dynamic-slice_fusion.3), kind=kOutput, calls=%fused_computation.28.clone.1 | convolution fusion | flops 537657344 | bytes 3145732 | tf_op jit(solution)/shard_map/while/body/eval_jaxpr/dot_general | solution.py:45
  188.6 2.1 copy.55
  190.7 19.5 %dynamic_update_slice.27 = f32[2,512,512]{2,0,1:T(2,128)} dynamic-update-slice(f32[2,512,512]{2,0,1:T(2,128)} %get-tuple-element.237, f32[1,512,512]{2,0,1:T(1,128)} %copy.55, s32[]{:T(128)S(6)} %copy.63, s32[]{:T(128)} %constant.97.clone.1..sunk, s32[]{:T(128)} %constant.97.clone.1..sunk) | dynamic-update-slice | bytes 2097156 | tf_op jit(solution)/shard_map/while/body/jit(dynamic_update_index_in_dim)/dynamic_update_slice | solution.py:74
  211.7 2.5 constant_dynamic-slice_fusion.3
  215.7 3.9 %multiply_reduce_fusion.10 = (f32[]{:T(128)}, f32[512,512]{1,0:T(8,128)S(1)}) fusion(f32[1,512,512]{2,0,1:T(1,128)S(1)} %constant_dynamic-slice_fusion.3, f32[2,512,512]{2,1,0:T(8,128)} %get-tuple-element.252, s32[]{:T(128)S(6)} %copy.63), kind=kOutput, calls=%fused_computation.32.clone.1 | convolution fusion | flops 1611923456 | bytes 3145736 | tf_op jit(solution)/shard_map/while/body/eval_jaxpr/dot_general | solution.py:34
  224.5 4.7 %multiply_reduce_fusion.9 = (f32[]{:T(128)}, f32[512,512]{1,0:T(8,128)}) fusion(f32[1,512,512]{2,0,1:T(1,128)S(1)} %constant_dynamic-slice_fusion.3, f32[2,512,512]{2,1,0:T(8,128)} %get-tuple-element.253, s32[]{:T(128)S(6)} %copy.63), kind=kOutput, calls=%fused_computation.30.clone.1 | convolution fusion | flops 1611923456 | bytes 3145736 | tf_op jit(solution)/shard_map/while/body/eval_jaxpr/dot_general | solution.py:37
  230.1 4.4 %convolution_convert_fusion.13 = bf16[512,512]{1,0:T(8,128)(2,1)} fusion(f32[512,512]{1,0:T(8,128)} %get-tuple-element.217, f32[]{:T(128)S(6)} %div.33), kind=kOutput, calls=%fused_computation.11.clone.1 | convolution fusion | flops 538968064 | bytes 1572868 | tf_op jit(solution)/shard_map/while/body/eval_jaxpr/dot_general | solution.py:10
  234.4 2.6 fusion.78
  237.1 2.9 convolution_convert_fusion.14
  240.0 3.4 %multiply_reduce_fusion.11 = (f32[]{:T(128)}, f32[512,512]{1,0:T(8,128)}) fusion(bf16[512,512]{1,0:T(8,128)(2,1)} %convolution_convert_fusion.14, bf16[512,512]{1,0:T(8,128)(2,1)S(1)} %convolution_convert_fusion.16, f32[1,512,512]{2,0,1:T(1,128)S(1)} %constant_dynamic-slice_fusion.3), kind=kOutput, calls=%fused_computation.28.clone.1 | convolution fusion | flops 537657344 | bytes 3145732 | tf_op jit(solution)/shard_map/while/body/eval_jaxpr/dot_general | solution.py:45
  245.4 2.1 copy.55
  247.5 19.5 %dynamic_update_slice.27 = f32[2,512,512]{2,0,1:T(2,128)} dynamic-update-slice(f32[2,512,512]{2,0,1:T(2,128)} %get-tuple-element.237, f32[1,512,512]{2,0,1:T(1,128)} %copy.55, s32[]{:T(128)S(6)} %copy.63, s32[]{:T(128)} %constant.97.clone.1..sunk, s32[]{:T(128)} %constant.97.clone.1..sunk) | dynamic-update-slice | bytes 2097156 | tf_op jit(solution)/shard_map/while/body/jit(dynamic_update_index_in_dim)/dynamic_update_slice | solution.py:74
  268.5 5.9 %all-to-all-start.1 = ((f32[1,2,512,512]{3,1,0,2:T(2,128)}), f32[1,2,512,512]{3,1,0,2:T(2,128)S(1)}, u32[]{:S(2)}, u32[]{:S(2)}) async-start(f32[1,2,512,512]{3,1,0,2:T(2,128)} %bitcast.98), calls=%async_computation.1 | async-start | bytes 4194304 | tf_op jit(solution)/shard_map/all_to_all | solution.py:77
  275.0 4.8 %multiply_bitcast_fusion.1 = (f32[1,1,2,512,512]{4,3,2,1,0:T(8,128)}, f32[1,1,2,512,512]{4,3,2,1,0:T(8,128)}) fusion(f32[2,512,512]{2,1,0:T(8,128)} %get-tuple-element.116, f32[2]{0:T(128)S(1)} %compare_convert_fusion, f32[2,512,512]{2,1,0:T(8,128)} %get-tuple-element.115), kind=kLoop, calls=%fused_computation.48 | loop fusion | flops 1048576 | bytes 8388616 | tf_op jit(solution)/shard_map/broadcast_in_dim | solution.py:80
  279.9 44.3 %all-to-all-done.1 = f32[1,2,512,512]{3,1,0,2:T(2,128)S(1)} async-done(((f32[1,2,512,512]{3,1,0,2:T(2,128)}), f32[1,2,512,512]{3,1,0,2:T(2,128)S(1)}, u32[]{:S(2)}, u32[]{:S(2)}) %all-to-all-start.1) | async-done | bytes 2097184 | tf_op jit(solution)/shard_map/all_to_all | solution.py:77
  324.1 2.1 copy.45
  326.2 2.7 reshape.31
  (27 shorter events, 20.2 us)
Async XLA Ops:
  0.6 2.2 copy-start
  10.4 62.7 %all-to-all-start = ((f32[64,2,8,512]{3,1,2,0:T(2,128)}), f32[64,2,8,512]{3,1,2,0:T(2,128)S(1)}, u32[]{:S(2)}, u32[]{:S(2)}) async-start(f32[64,2,8,512]{3,1,2,0:T(2,128)} %copy.18), calls=%async_computation | async-start | bytes 4194304 | tf_op jit(solution)/shard_map/all_to_all | solution.py:68
  188.6 21.6 %copy-start.1 = (f32[512,512]{1,0:T(8,128)S(1)}, f32[512,512]{1,0:T(8,128)}, u32[]{:S(2)}) copy-start(f32[512,512]{1,0:T(8,128)} %get-tuple-element.217) | copy-start | bytes 3145732 | tf_op jit(solution)/shard_map/while
  245.4 21.6 %copy-start.1 = (f32[512,512]{1,0:T(8,128)S(1)}, f32[512,512]{1,0:T(8,128)}, u32[]{:S(2)}) copy-start(f32[512,512]{1,0:T(8,128)} %get-tuple-element.217) | copy-start | bytes 3145732 | tf_op jit(solution)/shard_map/while
  268.5 55.6 %all-to-all-start.1 = ((f32[1,2,512,512]{3,1,0,2:T(2,128)}), f32[1,2,512,512]{3,1,0,2:T(2,128)S(1)}, u32[]{:S(2)}, u32[]{:S(2)}) async-start(f32[1,2,512,512]{3,1,0,2:T(2,128)} %bitcast.98), calls=%async_computation.1 | async-start | bytes 4194304 | tf_op jit(solution)/shard_map/all_to_all | solution.py:77
where the time goes:
time: 335 us; the launch traced here: 331 us
  waiting for transfers between devices  93.9 us (28%)
  blocking collectives  76.7 us (23%)
  local copies, waits for them, and re-layouts  62.1 us (19%)
  matrix products  55.7 us (17%)
  starting transfers between devices  18.9 us (6%)
  other arithmetic  16.3 us (5%)
  loops' own time  5.94 us (2%)
    psum x1, blocking collectives, local(): squares = lax.psum(jnp.sum(arrived * arrived), ('dp', 'tensor'))  76.7 us
    all_to_all x1, waiting for transfers between devices, local(): lax.all_to_all(packed, 'dp', split_axis=0, concat_axis=2, tiled=True)[0]  49.7 us
    dynamic_update_slice x6, local copies, waits for them, and re-layouts, local(): lax.map(update_slot, (clip_factor * arrived, left_state[0, 0], right_stat...  46.1 us
    all_to_all x1, waiting for transfers between devices, local(): lax.all_to_all(step_slots[None], 'dp', split_axis=2, concat_axis=0, tiled...  44.3 us
    dot_general x12, matrix products, product(): jnp.dot(left_op.astype(jnp.bfloat16), right_op.astype(jnp.bfloat16), pref...  28.2 us
    all_to_all x1, starting transfers between devices, local(): lax.all_to_all(packed, 'dp', split_axis=0, concat_axis=2, tiled=True)[0]  13 us
    dot_general x2, matrix products, update_slot(): lax.dot_general(clipped, clipped, (((0,), (0,)), ((), ())), precision=lax...  9.45 us
    dot_general x2, matrix products, update_slot(): lax.dot_general(clipped, clipped, (((1,), (1,)), ((), ())), precision=lax...  7.75 us
  transfers between devices with their start and end apart: 2, of which 2 were waited for; matrix products, arithmetic and copies ran while one was open for 2% of the time, Pallas kernels for 0%

commit v1 on v0

v1 whole, which is shorter than its diff:
```python
import functools

import jax
import jax.numpy as jnp
from jax import lax
from jax.experimental import pallas as pl
from jax.experimental.pallas import tpu as pltpu
from jax.sharding import PartitionSpec as P

MESH = pl.DeviceIdType.MESH
F32 = jnp.float32
BF16 = jnp.bfloat16


def matmul(a, b):
    return jnp.dot(a, b, preferred_element_type=F32)


def total(x):
    return jnp.sum(x, keepdims=True)


def scaled_root(factor, eye):
    scaling = 2.5 * lax.rsqrt(total(factor * factor) + 1e-06)
    matrix = scaling * factor
    step_one = jnp.where(eye, 1.25, 0.0) - 0.25 * matrix
    step_one = step_one.astype(BF16)
    square = matmul(step_one, step_one).astype(BF16)
    fourth = matmul(square, square).astype(BF16)
    matrix = matmul(fourth, matrix.astype(BF16))
    step_two = (jnp.where(eye, 1.25, 0.0) - 0.25 * matrix).astype(BF16)
    return matmul(step_one, step_two), scaling


def kernel(
    n_dp, n_tensor, blocks,
    source_ref, place_ref, filled_ref, grad_ref, left_ref, right_ref,
    step_ref, new_left_ref, new_right_ref,
    packed, arrived, left, right, steps, returned, sums_y, sums_p, sums_z, mine_y, mine_p, mine_z,
    state_sem, out_sem, send_sem, recv_sem, back_send, back_recv, sum_send, sum_recv,
):
    me = lax.axis_index("dp")
    tensor = lax.axis_index("tensor")
    slots = arrived.shape[0]
    plane = 8
    depth = n_dp // plane
    my_z = me // plane
    my_p = lax.rem(me, plane)
    order = arrived.shape[1] * arrived.shape[2]

    for slot in range(slots):
        pltpu.make_async_copy(left_ref.at[slot], left.at[slot], state_sem.at[0, slot]).start()
        pltpu.make_async_copy(right_ref.at[slot], right.at[slot], state_sem.at[1, slot]).start()

    barrier = pltpu.get_barrier_semaphore()

    def greet(i, _):
        pl.semaphore_signal(barrier, inc=1, device_id=(lax.rem(me + i, n_dp), tensor), device_id_type=MESH)
        return 0

    lax.fori_loop(1, n_dp, greet, 0)
    for i in range(1, n_tensor):
        pl.semaphore_signal(barrier, inc=1, device_id=(me, lax.rem(tensor + i, n_tensor)), device_id_type=MESH)

    grads = grad_ref[...]
    squares = jnp.sum(grads * grads, axis=0)
    tile = squares[:, :128]
    for i in range(1, squares.shape[1] // 128):
        tile = tile + squares[:, i * 128:(i + 1) * 128]
    mine_y[...] = tile
    sums_y[tensor] = tile

    def pack(q, _):
        for slot in range(slots):
            packed[slot, q] = grad_ref[source_ref[slot * n_dp + q]]
        return 0

    lax.fori_loop(0, n_dp, pack, 0)
    pl.semaphore_wait(barrier, n_dp - 1 + n_tensor - 1)

    def peer(i):
        z = lax.rem(my_z + lax.rem(i, depth), depth)
        p = lax.rem(my_p + i // depth, plane)
        return z * plane + p

    def tell(src, dst, stage, device):
        pltpu.make_async_remote_copy(
            src_ref=src, dst_ref=dst, send_sem=sum_send.at[stage], recv_sem=sum_recv.at[stage],
            device_id=device, device_id_type=MESH,
        ).start()

    def heard(sums, stage, count):
        others = sums.at[pl.ds(0, count)]
        pltpu.make_async_copy(others, others, sum_recv.at[stage]).wait()
        pltpu.make_async_copy(others, others, sum_send.at[stage]).wait()

    def send_slot(slot):
        def go(i, _):
            to = peer(i)
            pltpu.make_async_remote_copy(
                src_ref=packed.at[slot, to], dst_ref=arrived.at[slot, me],
                send_sem=send_sem.at[slot], recv_sem=recv_sem.at[slot],
                device_id=(to, tensor), device_id_type=MESH,
            ).start()
            return 0

        lax.fori_loop(1, n_dp, go, 0)
        pltpu.make_async_copy(packed.at[slot, me], arrived.at[slot, me], recv_sem.at[slot]).start()

    for i in range(1, n_tensor):
        tell(mine_y, sums_y.at[tensor], 0, (me, lax.rem(tensor + i, n_tensor)))
    send_slot(0)
    heard(sums_y, 0, n_tensor - 1)
    tile = jnp.sum(sums_y[...], axis=0)
    mine_p[...] = tile
    sums_p[my_p] = tile
    for i in range(1, plane):
        tell(mine_p, sums_p.at[my_p], 1, (my_z * plane + lax.rem(my_p + i, plane), tensor))
    for slot in range(1, slots):
        send_slot(slot)
    heard(sums_p, 1, plane - 1)
    tile = jnp.sum(sums_p[...], axis=0)
    mine_z[...] = tile
    sums_z[my_z] = tile
    for i in range(1, depth):
        tell(mine_z, sums_z.at[my_z], 2, (lax.rem(my_z + i, depth) * plane + my_p, tensor))
    heard(sums_z, 2, depth - 1)
    entries = blocks * n_tensor * order * order
    clip = lax.rsqrt(total(jnp.sum(sums_z[...], axis=0)) / entries + 1e-06)
    clip_sq = clip * clip

    eye = lax.broadcasted_iota(jnp.int32, (order, order), 0) == lax.broadcasted_iota(jnp.int32, (order, order), 1)

    def update(slot, _):
        filled = filled_ref[slot]
        pltpu.make_async_copy(arrived.at[slot], arrived.at[slot], recv_sem.at[slot]).wait()
        pltpu.make_async_copy(left.at[slot], left.at[slot], state_sem.at[0, slot]).wait()
        pltpu.make_async_copy(right.at[slot], right.at[slot], state_sem.at[1, slot]).wait()
        grad = arrived[slot].reshape(order, order)
        grad_sq = total(grad * grad)
        grad = grad.astype(BF16)
        gram = clip_sq * (0.1 / order)
        left_new = 0.9 * left[slot] + gram * lax.dot_general(
            grad, grad, (((1,), (1,)), ((), ())), preferred_element_type=F32)
        left[slot] = filled * left_new
        right_new = 0.9 * right[slot] + gram * lax.dot_general(
            grad, grad, (((0,), (0,)), ((), ())), preferred_element_type=F32)
        right[slot] = filled * right_new
        pltpu.make_async_copy(left.at[slot], new_left_ref.at[slot], out_sem.at[0, slot]).start()
        pltpu.make_async_copy(right.at[slot], new_right_ref.at[slot], out_sem.at[1, slot]).start()
        left_root, left_scale = scaled_root(left_new, eye)
        right_root, right_scale = scaled_root(right_new, eye)
        middle = matmul(left_root.astype(BF16), grad).astype(BF16)
        direction = matmul(middle, right_root.astype(BF16))
        scale = clip * jnp.sqrt(jnp.sqrt(left_scale * right_scale))
        ratio = jnp.sqrt(clip_sq * grad_sq + 1e-06) * lax.rsqrt(scale * scale * total(direction * direction) + 1e-06)
        steps[slot] = ((-ratio * scale) * direction).reshape(n_dp, order // n_dp, order)

        def back(i, _):
            to = peer(i)
            pltpu.make_async_remote_copy(
                src_ref=steps.at[slot, to], dst_ref=returned.at[slot, me],
                send_sem=back_send.at[slot], recv_sem=back_recv.at[slot],
                device_id=(to, tensor), device_id_type=MESH,
            ).start()
            return 0

        lax.fori_loop(1, n_dp, back, 0)
        pltpu.make_async_copy(steps.at[slot, me], returned.at[slot, me], back_recv.at[slot]).start()
        return 0

    lax.fori_loop(0, slots, update, 0)

    for slot in range(slots):
        others = packed.at[slot, pl.ds(0, n_dp - 1)]
        pltpu.make_async_copy(others, others, send_sem.at[slot]).wait()
        pltpu.make_async_copy(left.at[slot], new_left_ref.at[slot], out_sem.at[0, slot]).wait()
        pltpu.make_async_copy(right.at[slot], new_right_ref.at[slot], out_sem.at[1, slot]).wait()
    for slot in range(slots):
        pltpu.make_async_copy(returned.at[slot], returned.at[slot], back_recv.at[slot]).wait()
        others = steps.at[slot, pl.ds(0, n_dp - 1)]
        pltpu.make_async_copy(others, others, back_send.at[slot]).wait()

    def pick(j, _):
        step_ref[j] = returned[place_ref[blocks + j], place_ref[j]]
        return 0

    lax.fori_loop(0, blocks, pick, 0)


def local(grad_blocks, owner_map, left_state, right_state):
    blocks, rows, order = grad_blocks.shape
    slots = left_state.shape[2]
    n_dp = lax.axis_size("dp")
    n_tensor = lax.axis_size("tensor")
    owners = lax.dynamic_slice_in_dim(owner_map, lax.axis_index("tensor"), 1, 0)[0]
    positions = jnp.arange(blocks, dtype=jnp.int32)
    same_owner = owners[:, None] == owners[None, :]
    earlier = positions[:, None] < positions[None, :]
    slot_of = jnp.sum(jnp.where(same_owner & earlier, 1, 0), axis=0).astype(jnp.int32)
    target = slot_of * n_dp + owners
    hit = jnp.arange(slots * n_dp, dtype=jnp.int32)[None, :] == target[:, None]
    source = jnp.sum(jnp.where(hit, positions[:, None], 0), axis=0).astype(jnp.int32)
    place = jnp.concatenate([owners, slot_of])
    owned = jnp.sum(jnp.where(owners == lax.axis_index("dp"), 1, 0))
    filled = (jnp.arange(slots) < owned).astype(F32)

    smem = pl.BlockSpec(memory_space=pltpu.SMEM)
    vmem = pl.BlockSpec(memory_space=pltpu.VMEM)
    hbm = pl.BlockSpec(memory_space=pl.ANY)
    step_blocks, new_left, new_right = pl.pallas_call(
        functools.partial(kernel, n_dp, n_tensor, blocks),
        out_shape=(
            jax.ShapeDtypeStruct((blocks, rows, order), F32),
            jax.ShapeDtypeStruct((slots, order, order), F32),
            jax.ShapeDtypeStruct((slots, order, order), F32),
        ),
        in_specs=[smem, smem, smem, vmem, hbm, hbm],
        out_specs=(vmem, hbm, hbm),
        scratch_shapes=[
            pltpu.VMEM((slots, n_dp, rows, order), F32),
            pltpu.VMEM((slots, n_dp, rows, order), F32),
            pltpu.VMEM((slots, order, order), F32),
            pltpu.VMEM((slots, order, order), F32),
            pltpu.VMEM((slots, n_dp, rows, order), F32),
            pltpu.VMEM((slots, n_dp, rows, order), F32),
            pltpu.VMEM((n_tensor, 8, 128), F32),
            pltpu.VMEM((8, 8, 128), F32),
            pltpu.VMEM((n_dp // 8, 8, 128), F32),
            pltpu.VMEM((8, 128), F32),
            pltpu.VMEM((8, 128), F32),
            pltpu.VMEM((8, 128), F32),
            pltpu.SemaphoreType.DMA((2, slots)),
            pltpu.SemaphoreType.DMA((2, slots)),
            pltpu.SemaphoreType.DMA((slots,)),
            pltpu.SemaphoreType.DMA((slots,)),
            pltpu.SemaphoreType.DMA((slots,)),
            pltpu.SemaphoreType.DMA((slots,)),
            pltpu.SemaphoreType.DMA((3,)),
            pltpu.SemaphoreType.DMA((3,)),
        ],
        compiler_params=pltpu.CompilerParams(
            collective_id=0, has_side_effects=True, vmem_limit_bytes=48 * 2**20
        ),
        cost_estimate=pl.CostEstimate(flops=slots * 24 * order**3, bytes_accessed=18 * order * order, transcendentals=0),
    )(source, place, filled, grad_blocks, left_state[0, 0], right_state[0, 0])
    return (step_blocks, new_left[None, None], new_right[None, None])


def solution(mesh):
    state = P("tensor", "dp", None, None, None)
    return jax.shard_map(
        local,
        mesh=mesh,
        in_specs=(P("tensor", "dp", None), P(), state, state),
        out_specs=(P("tensor", "dp", None), state, state),
        check_vma=False,
    )
```

time: 335 us -> 122 us (0.36); the launches traced: 331 us -> 122 us
  Pallas kernels: 0 us -> 114 us
  waiting for transfers between devices: 93.9 us -> 0 us
  blocking collectives: 76.7 us -> 0 us
  local copies, waits for them, and re-layouts: 62.1 us -> 4.47 us
  matrix products: 55.7 us -> 0 us
  starting transfers between devices: 18.9 us -> 0 us
  other arithmetic: 16.3 us -> 2.24 us
  loops' own time: 5.94 us -> 0 us
    pallas_call x0 -> x1, Pallas kernels: none -> 114 us  [local(): pl.pallas_call(functools.partial(kernel, n_dp, n_tensor, blocks), out_sha...]
    all_to_all x2 -> x0, waiting for transfers between devices: 93.9 us -> none  [the longest x1 49.7 us: local(): lax.all_to_all(packed, 'dp', split_axis=0, concat_axis=2, tiled=True)[0]]
    psum x1 -> x0, blocking collectives: 76.7 us -> none  [local(): squares = lax.psum(jnp.sum(arrived * arrived), ('dp', 'tensor'))]
    dot_general x20 -> x0, matrix products: 55.7 us -> none  [the longest x12 28.2 us: product(): jnp.dot(left_op.astype(jnp.bfloat16), right_op.astype(jnp.bfloat16), pref...]
    dynamic_update_slice x6 -> x0, local copies, waits for them, and re-layouts: 46.1 us -> none  [local(): lax.map(update_slot, (clip_factor * arrived, left_state[0, 0], right_stat...]
    all_to_all x2 -> x0, starting transfers between devices: 18.9 us -> none  [the longest x1 13 us: local(): lax.all_to_all(packed, 'dp', split_axis=0, concat_axis=2, tiled=True)[0]]
    reshape x3 -> x0, local copies, waits for them, and re-layouts: 7.75 us -> none  [the longest x2 5.06 us: local(): packed = packed.reshape(dp_size, slot_count, rows_dev, block_order)]
    broadcast_in_dim x3 -> x0, other arithmetic: 7.47 us -> none  [the longest x1 4.84 us: local(): (filled * right_new)[None, None]]
  transfers between devices with their start and end apart: 2 -> 0, of which waited for: 2 -> 0; matrix products, arithmetic and copies ran while one was open for 2% -> 0% of each run, Pallas kernels for 0% -> 0%
where the time goes in v1:
time: 122 us
  Pallas kernels  114 us (93%)
  local copies, waits for them, and re-layouts  4.47 us (4%)
  other arithmetic  2.24 us (2%)
    pallas_call x1, Pallas kernels, local(): pl.pallas_call(functools.partial(kernel, n_dp, n_tensor, blocks), out_sha...  114 us
    unnamed x5, local copies, waits for them, and re-layouts  4.47 us

profile of v1, /device:TPU:1, one launch (start us, length us, event | category | flops | bytes accessed | tf_op | source)
XLA Modules:
  0.0 121.7 jit_solution(18394382576418410614)
XLA Ops:
  0.6 1.3 %fusion.1 = (s32[]{:T(128)}, s32[32]{0:T(128)S(1)}) fusion(s32[]{:T(128)S(6)} %axis_index.25, s32[4,32]{1,0:T(4,128)} %param.5, s32[]{:T(128)S(6)} %select_n.15), kind=kLoop, calls=%fused_computation.7 | loop fusion | flops 95 | bytes 268 | tf_op jit(solution)/shard_map/reduce_sum | solution.py:205
  2.0 0.1 select_reduce_fusion.1
  2.1 0.1 pad_add_fusion.place_ref
  2.1 0.1 select_reduce_fusion.source_ref
  2.2 0.6 compare_convert_fusion.filled_ref
  2.9 0.0 copy-start
  2.9 1.0 copy-done
  3.9 114.3 %shard_map.67 = (f32[32,8,512]{2,1,0:T(8,128)S(1)}, f32[2,512,512]{2,1,0:T(8,128)S(1)}, f32[2,512,512]{2,1,0:T(8,128)S(1)}) custom-call(s32[128]{0:T(128)S(1)} %select_reduce_fusion.source_ref, s32[64]{0:T(128)S(1)} %pad_add_fusion.place_ref, f32[2]{0:T(128)S(1)} %compare_convert_fusion.filled_ref, f32[32,8,512]{2,1,0:T(8,128)S(1)} %copy-done, ...), custom_call_target="tpu_custom_call" | custom-call | flops 6442450944 | bytes 4718592 | tf_op jit(solution)/shard_map/pallas_call | solution.py:211
  118.3 0.8 copy.10
  119.1 1.3 %copy.11 = f32[1,1,2,512,512]{4,3,2,1,0:T(8,128)} copy(f32[1,1,2,512,512]{4,3,2,1,0:T(8,128)S(1)} %bitcast.8) | data formatting | bytes 4194304
  120.4 1.3 %copy.12 = f32[1,1,2,512,512]{4,3,2,1,0:T(8,128)} copy(f32[1,1,2,512,512]{4,3,2,1,0:T(8,128)S(1)} %bitcast.7) | data formatting | bytes 4194304
  (1 shorter events, 0.0 us)
Async XLA Ops:
  2.9 1.0 copy-start

commit v2 on v1

v2 whole, which is shorter than its diff:
```python
import functools

import jax
import jax.numpy as jnp
from jax import lax
from jax.experimental import pallas as pl
from jax.experimental.pallas import tpu as pltpu
from jax.sharding import PartitionSpec as P

MESH = pl.DeviceIdType.MESH
F32 = jnp.float32
BF16 = jnp.bfloat16
I32 = jnp.int32
PLANE = 8
BUNDLE = 4


def matmul(a, b):
    return jnp.dot(a, b, preferred_element_type=F32)


def total(x):
    return jnp.sum(x, keepdims=True)


def scaled_root(factor, eye):
    scaling = 2.5 * lax.rsqrt(total(factor * factor) + 1e-06)
    matrix = scaling * factor
    step_one = jnp.where(eye, 1.25, 0.0) - 0.25 * matrix
    step_one = step_one.astype(BF16)
    square = matmul(step_one, step_one).astype(BF16)
    fourth = matmul(square, square).astype(BF16)
    matrix = matmul(fourth, matrix.astype(BF16))
    step_two = (jnp.where(eye, 1.25, 0.0) - 0.25 * matrix).astype(BF16)
    return matmul(step_one, step_two), scaling


def plan(owners, me, n_dp, bundled):
    blocks = owners.shape[1]
    sub = lax.broadcasted_iota(I32, (blocks, blocks), 0)
    lane = lax.broadcasted_iota(I32, (blocks, blocks), 1)
    across = jnp.broadcast_to(owners, (blocks, blocks))

    def column(row):
        return jnp.sum(jnp.where(sub == lane, row, 0), axis=1, keepdims=True)

    owner = column(across)
    same = across == owner
    slot = jnp.sum(jnp.where(same & (lane < sub), 1, 0), axis=1, keepdims=True)
    slot_row = jnp.sum(jnp.where(same & (sub < lane), 1, 0), axis=0, keepdims=True)
    depth_of, place_of = owner // PLANE, owner % PLANE
    second_row = jnp.broadcast_to(jnp.where(slot_row == 1, owners, n_dp * 2), (blocks, blocks))
    rank = jnp.sum(jnp.where((second_row // PLANE == depth_of) & (second_row < owner), 1, 0), axis=1, keepdims=True)
    key = jnp.where(slot == 1, depth_of * BUNDLE + rank, -1)
    wide = lax.broadcasted_iota(I32, (blocks, 128), 1)
    block = lax.broadcasted_iota(I32, (blocks, 128), 0)

    def row(value):
        return jnp.sum(value, axis=0, keepdims=True)

    first_of = row(jnp.where((slot == 0) & (owner == wide), block, 0))
    second_of = row(jnp.where((slot == 1) & (owner == wide), block, 0))
    bundle_of = row(jnp.where(key == wide, block, 0))
    rank_of = row(jnp.where((slot == 1) & (owner == wide), rank, 0))
    place_at = row(jnp.where(key == wide, place_of, 0))
    found = jnp.where(slot == 1, n_dp + (key if bundled else owner), owner)
    pick = row(jnp.where(block == wide, found, 0))
    owned = jnp.sum(jnp.where(owners == me, 1, 0), keepdims=True)
    return (first_of, second_of, bundle_of, rank_of, place_at, pick), owned


FIRST, SECOND, BUNDLED, RANK, PLACE, PICK = range(6)


def kernel(
    n_dp, n_tensor, bundled,
    owner_ref, grad_ref, left_ref, right_ref,
    step_ref, new_left_ref, new_right_ref,
    grads, packed, arrived, left, right, steps, returned, z_out, z_in, x_back, z_back,
    sums_z, sums_p, sums_y, mine_z, mine_p, mine_y, rows_v, rows_s,
    local_sem, state_sem, out_sem, send_sem, recv_sem, back_send, back_recv, hop_send, hop_recv, sum_send, sum_recv,
):
    me = lax.axis_index("dp")
    tensor = lax.axis_index("tensor")
    blocks = grads.shape[0]
    slots, depth = arrived.shape[:2]
    rows, order = grads.shape[1:]
    my_z = me // PLANE
    my_p = lax.rem(me, PLANE)

    get_grads = pltpu.make_async_copy(grad_ref, grads, local_sem.at[0])
    get_grads.start()

    barrier = pltpu.get_barrier_semaphore()

    def greet(i, _):
        pl.semaphore_signal(barrier, inc=1, device_id=(lax.rem(me + i, n_dp), tensor), device_id_type=MESH)
        return 0

    lax.fori_loop(1, n_dp, greet, 0)
    for i in range(1, n_tensor):
        pl.semaphore_signal(barrier, inc=1, device_id=(me, lax.rem(tensor + i, n_tensor)), device_id_type=MESH)

    tables, owned = plan(owner_ref[pl.ds(tensor, 1), :], me, n_dp, bundled)
    rows_v[...] = jnp.concatenate(tables + (tables[0], tables[0]), axis=0)
    put_rows = pltpu.make_async_copy(rows_v, rows_s, local_sem.at[1])
    put_rows.start()
    for slot in range(slots):
        pltpu.make_async_copy(left_ref.at[slot], left.at[slot], state_sem.at[0, slot]).start()
        pltpu.make_async_copy(right_ref.at[slot], right.at[slot], state_sem.at[1, slot]).start()

    get_grads.wait()
    tile = jnp.zeros((8, 128), F32)
    for k in range(order // 128):
        part = grads[:, :, k * 128:(k + 1) * 128]
        tile = tile + jnp.sum(part * part, axis=0)
    mine_z[...] = tile
    sums_z[my_z] = tile
    put_rows.wait()

    if bundled:
        def pack_bundle(q, _):
            z_out[q] = grads[rows_s[BUNDLED, q]]
            return 0

        lax.fori_loop(0, depth * BUNDLE, pack_bundle, 0)

    def pack(q, _):
        z, p = q // PLANE, lax.rem(q, PLANE)
        packed[0, z, p] = grads[rows_s[FIRST, q]]
        if not bundled:
            packed[1, z, p] = grads[rows_s[SECOND, q]]
        return 0

    lax.fori_loop(0, n_dp, pack, 0)
    pl.semaphore_wait(barrier, n_dp - 1 + n_tensor - 1)

    def copy(src, dst, send, recv, to):
        pltpu.make_async_remote_copy(
            src_ref=src, dst_ref=dst, send_sem=send, recv_sem=recv, device_id=to, device_id_type=MESH
        ).start()

    def wait(ref, sem):
        pltpu.make_async_copy(ref, ref, sem).wait()

    def peer(i):
        return lax.rem(my_z + lax.rem(i, depth), depth), lax.rem(my_p + i // depth, PLANE)

    def along_z(i):
        return lax.rem(my_z + i, depth)

    def in_plane(i):
        return lax.rem(my_p + i, PLANE)

    def heard(sums, stage, count):
        wait(sums.at[pl.ds(0, count)], sum_recv.at[stage])
        wait(sums.at[pl.ds(0, count)], sum_send.at[stage])
        return jnp.sum(sums[...], axis=0)

    def dispatch(slot, start, stop):
        def go(i, _):
            z, p = peer(i)
            copy(packed.at[slot, z, p], arrived.at[slot, my_z, my_p], send_sem.at[slot], recv_sem.at[slot],
                 (z * PLANE + p, tensor))
            return 0

        lax.fori_loop(start, stop, go, 0)

    def give_back(start, stop, slot):
        def go(i, _):
            z, p = peer(i)
            copy(steps.at[slot, z, p], returned.at[slot * n_dp + me], back_send.at[slot], back_recv.at[slot],
                 (z * PLANE + p, tensor))
            return 0

        lax.fori_loop(start, stop, go, 0)

    for i in range(1, depth):
        copy(mine_z, sums_z.at[my_z], sum_send.at[0], sum_recv.at[0], (along_z(i) * PLANE + my_p, tensor))
    if bundled:
        for i in range(1, depth):
            z = along_z(i)
            copy(z_out.at[pl.ds(z * BUNDLE, BUNDLE)], z_in.at[pl.ds(my_z * BUNDLE, BUNDLE)], hop_send.at[0], hop_recv.at[0],
                 (z * PLANE + my_p, tensor))
        pltpu.make_async_copy(
            z_out.at[pl.ds(my_z * BUNDLE, BUNDLE)], z_in.at[pl.ds(my_z * BUNDLE, BUNDLE)], hop_recv.at[0]).start()
    pltpu.make_async_copy(packed.at[0, my_z, my_p], arrived.at[0, my_z, my_p], recv_sem.at[0]).start()
    dispatch(0, 1, n_dp // 2)
    tile = heard(sums_z, 0, depth - 1)
    mine_p[...] = tile
    sums_p[my_p] = tile
    for i in range(1, PLANE):
        copy(mine_p, sums_p.at[my_p], sum_send.at[1], sum_recv.at[1], (my_z * PLANE + in_plane(i), tensor))
    if bundled:
        wait(z_in, hop_recv.at[0])

        def spread(p, _):
            rank = rows_s[RANK, my_z * PLANE + p]
            for z in range(depth):
                packed[1, z, p] = z_in[z * BUNDLE + rank]
            return 0

        lax.fori_loop(0, PLANE, spread, 0)
        for i in range(1, PLANE):
            p = in_plane(i)
            copy(packed.at[1, pl.ds(0, depth), p], arrived.at[1, pl.ds(0, depth), my_p], send_sem.at[1], recv_sem.at[1],
                 (my_z * PLANE + p, tensor))
        pltpu.make_async_copy(
            packed.at[1, pl.ds(0, depth), my_p], arrived.at[1, pl.ds(0, depth), my_p], recv_sem.at[1]).start()
    else:
        dispatch(1, 1, n_dp)
        pltpu.make_async_copy(packed.at[1, my_z, my_p], arrived.at[1, my_z, my_p], recv_sem.at[1]).start()
    dispatch(0, n_dp // 2, n_dp)
    tile = heard(sums_p, 1, PLANE - 1)
    mine_y[...] = tile
    sums_y[tensor] = tile
    for i in range(1, n_tensor):
        copy(mine_y, sums_y.at[tensor], sum_send.at[2], sum_recv.at[2], (me, lax.rem(tensor + i, n_tensor)))
    tile = heard(sums_y, 2, n_tensor - 1)
    clip = lax.rsqrt(total(tile) / (blocks * n_tensor * order * order) + 1e-06)
    clip_sq = clip * clip

    eye = lax.broadcasted_iota(I32, (order, order), 0) == lax.broadcasted_iota(I32, (order, order), 1)

    def update(k, _):
        slot = slots - 1 - k
        filled = jnp.where(owned > slot, 1.0, 0.0)
        wait(arrived.at[slot], recv_sem.at[slot])
        wait(left.at[slot], state_sem.at[0, slot])
        wait(right.at[slot], state_sem.at[1, slot])
        grad = arrived[slot].reshape(order, order)
        grad_sq = total(grad * grad)
        grad = grad.astype(BF16)
        gram = clip_sq * (0.1 / order)
        left_new = 0.9 * left[slot] + gram * lax.dot_general(
            grad, grad, (((1,), (1,)), ((), ())), preferred_element_type=F32)
        left[slot] = filled * left_new
        right_new = 0.9 * right[slot] + gram * lax.dot_general(
            grad, grad, (((0,), (0,)), ((), ())), preferred_element_type=F32)
        right[slot] = filled * right_new
        pltpu.make_async_copy(left.at[slot], new_left_ref.at[slot], out_sem.at[0, slot]).start()
        pltpu.make_async_copy(right.at[slot], new_right_ref.at[slot], out_sem.at[1, slot]).start()
        left_root, left_scale = scaled_root(left_new, eye)
        right_root, right_scale = scaled_root(right_new, eye)
        middle = matmul(left_root.astype(BF16), grad).astype(BF16)
        direction = matmul(middle, right_root.astype(BF16))
        scale = clip * jnp.sqrt(jnp.sqrt(left_scale * right_scale))
        ratio = jnp.sqrt(clip_sq * grad_sq + 1e-06) * lax.rsqrt(scale * scale * total(direction * direction) + 1e-06)
        steps[slot] = ((-ratio * scale) * direction).reshape(depth, PLANE, rows, order)

        @pl.when(k == 0)
        def _():
            if bundled:
                for i in range(1, PLANE):
                    p = in_plane(i)
                    copy(steps.at[1, pl.ds(0, depth), p], x_back.at[my_p], back_send.at[1], back_recv.at[1],
                         (my_z * PLANE + p, tensor))
                pltpu.make_async_copy(steps.at[1, pl.ds(0, depth), my_p], x_back.at[my_p], back_recv.at[1]).start()
            else:
                give_back(1, n_dp, 1)
                pltpu.make_async_copy(steps.at[1, my_z, my_p], returned.at[n_dp + me], back_recv.at[1]).start()

        return 0

    lax.fori_loop(0, slots, update, 0)

    pltpu.make_async_copy(steps.at[0, my_z, my_p], returned.at[me], back_recv.at[0]).start()
    give_back(1, n_dp // 2, 0)
    if bundled:
        wait(x_back, back_recv.at[1])

        def gather(q, _):
            place = rows_s[PLACE, my_z * BUNDLE + q]
            for z in range(depth):
                z_back[z * BUNDLE + q] = x_back[place, z]
            return 0

        lax.fori_loop(0, BUNDLE, gather, 0)
        for i in range(1, depth):
            z = along_z(i)
            copy(z_back.at[pl.ds(z * BUNDLE, BUNDLE)], returned.at[pl.ds(n_dp + my_z * BUNDLE, BUNDLE)],
                 hop_send.at[1], hop_recv.at[1], (z * PLANE + my_p, tensor))
        pltpu.make_async_copy(
            z_back.at[pl.ds(my_z * BUNDLE, BUNDLE)], returned.at[pl.ds(n_dp + my_z * BUNDLE, BUNDLE)], hop_recv.at[1]).start()
    give_back(n_dp // 2, n_dp, 0)

    others = returned.at[pl.ds(0, n_dp - 1)]
    wait(others, send_sem.at[0])
    if bundled:
        wait(z_out.at[pl.ds(0, (depth - 1) * BUNDLE)], hop_send.at[0])
        wait(x_back.at[pl.ds(0, PLANE - 1)], send_sem.at[1])
        wait(x_back.at[pl.ds(0, PLANE - 1)], back_send.at[1])
    else:
        wait(others, send_sem.at[1])
        wait(others, back_send.at[1])
    for slot in range(slots):
        pltpu.make_async_copy(left.at[slot], new_left_ref.at[slot], out_sem.at[0, slot]).wait()
        pltpu.make_async_copy(right.at[slot], new_right_ref.at[slot], out_sem.at[1, slot]).wait()
    wait(others, back_send.at[0])
    if bundled:
        wait(z_out.at[pl.ds(0, (depth - 1) * BUNDLE)], hop_send.at[1])
        wait(returned.at[pl.ds(n_dp, depth * BUNDLE)], hop_recv.at[1])
    else:
        wait(returned.at[pl.ds(n_dp, n_dp)], back_recv.at[1])
    wait(returned.at[pl.ds(0, n_dp)], back_recv.at[0])

    def pick(j, _):
        step_ref[j] = returned[rows_s[PICK, j]]
        return 0

    lax.fori_loop(0, blocks, pick, 0)


def owner_step(n_dp, n_tensor, bundled, owner_map, grads, left_old, right_old):
    blocks, rows, order = grads.shape
    slots = left_old.shape[0]
    depth = n_dp // PLANE
    vmem = pl.BlockSpec(memory_space=pltpu.VMEM)
    hbm = pl.BlockSpec(memory_space=pl.ANY)
    tile = pltpu.VMEM((8, 128), F32)
    state = pltpu.VMEM((slots, order, order), F32)
    parts = pltpu.VMEM((slots, depth, PLANE, rows, order), F32)
    bundles = pltpu.VMEM((depth * BUNDLE, rows, order), F32)
    dma = pltpu.SemaphoreType.DMA
    return pl.pallas_call(
        functools.partial(kernel, n_dp, n_tensor, bundled),
        out_shape=(
            jax.ShapeDtypeStruct((blocks, rows, order), F32),
            jax.ShapeDtypeStruct((slots, order, order), F32),
            jax.ShapeDtypeStruct((slots, order, order), F32),
        ),
        in_specs=[vmem, hbm, hbm, hbm],
        out_specs=(vmem, hbm, hbm),
        scratch_shapes=[
            pltpu.VMEM((blocks, rows, order), F32),
            parts, parts, state, state, parts,
            pltpu.VMEM((slots * n_dp, rows, order), F32),
            bundles, bundles,
            pltpu.VMEM((PLANE, depth, rows, order), F32),
            bundles,
            pltpu.VMEM((depth, 8, 128), F32),
            pltpu.VMEM((PLANE, 8, 128), F32),
            pltpu.VMEM((n_tensor, 8, 128), F32),
            tile, tile, tile,
            pltpu.VMEM((8, 128), I32),
            pltpu.SMEM((8, 128), I32),
            dma((2,)), dma((2, slots)), dma((2, slots)),
            dma((slots,)), dma((slots,)), dma((slots,)), dma((slots,)),
            dma((2,)), dma((2,)), dma((3,)), dma((3,)),
        ],
        compiler_params=pltpu.CompilerParams(
            collective_id=0 if bundled else 1, has_side_effects=True, vmem_limit_bytes=48 * 2**20
        ),
        cost_estimate=pl.CostEstimate(
            flops=slots * 24 * order**3, bytes_accessed=18 * order * order, transcendentals=0),
    )(owner_map, grads, left_old, right_old)


def local(grad_blocks, owner_map, left_state, right_state):
    n_dp = lax.axis_size("dp")
    n_tensor = lax.axis_size("tensor")
    blocks = owner_map.shape[1]
    positions = jnp.arange(blocks)
    twice = (owner_map[:, :, None] == owner_map[:, None, :]) & (positions[:, None] < positions[None, :])
    at = owner_map[:, None, :, None] // PLANE == jnp.arange(n_dp // PLANE)[None, None, None, :]
    seconds = jnp.sum(jnp.where(twice[:, :, :, None] & at, 1, 0), axis=(1, 2))
    step_blocks, new_left, new_right = lax.cond(
        jnp.max(seconds) <= BUNDLE,
        functools.partial(owner_step, n_dp, n_tensor, True),
        functools.partial(owner_step, n_dp, n_tensor, False),
        owner_map, grad_blocks, left_state[0, 0], right_state[0, 0],
    )
    return (step_blocks, new_left[None, None], new_right[None, None])


def solution(mesh):
    state = P("tensor", "dp", None, None, None)
    return jax.shard_map(
        local,
        mesh=mesh,
        in_specs=(P("tensor", "dp", None), P(), state, state),
        out_specs=(P("tensor", "dp", None), state, state),
        check_vma=False,
    )
```

time: 122 us -> 102 us (0.84)
  the two profiles are of different devices: /device:TPU:1 before, /device:TPU:16 now
where the time goes in v2:
time: 102 us
  Pallas kernels  94.7 us (93%)
  local copies, waits for them, and re-layouts  3.43 us (3%)
  other arithmetic  2.42 us (2%)
  between operations  1.3 us (1%)
    pallas_call x1, Pallas kernels, owner_step(): pl.pallas_call(functools.partial(kernel, n_dp, n_tensor, bundled), out_sh...  94.7 us
    unnamed x3, local copies, waits for them, and re-layouts  3.43 us

profile of v2, /device:TPU:16, one launch (start us, length us, event | category | flops | bytes accessed | tf_op | source)
XLA Modules:
  0.0 101.9 jit_solution(13586590249164792609)
XLA Ops:
  0.6 0.7 add_select_fusion
  1.3 0.8 compare_and_fusion
  2.2 0.2 select_reduce_fusion
  2.4 0.6 reduce_max.9
  3.7 94.7 %conditional.1 = ((f32[32,8,512]{2,1,0:T(8,128)S(1)}, f32[2,512,512]{2,1,0:T(8,128)S(1)}, f32[2,512,512]{2,1,0:T(8,128)S(1)})) conditional(s32[]{:T(128)} %convert_element_type.3, (s32[4,32]{1,0:T(4,128)}, f32[32,8,512]{2,1,0:T(8,128)}, f32[2,512,512]{2,1,0:T(8,128)}, f32[2,512,512]{2,1,0:T(8,128)}) %tuple.31, (s32[4,32]{1,0:T(4,128)}, ...), branch_computations={%region_2.3_spmd, %region_3.4_spmd} | conditional | flops 6442450944 | bytes 4718600 | solution.py:367
  3.7 94.7 %branch_1_fun.1 = (f32[32,8,512]{2,1,0:T(8,128)S(1)}, f32[2,512,512]{2,1,0:T(8,128)S(1)}, f32[2,512,512]{2,1,0:T(8,128)S(1)}) custom-call(s32[4,32]{1,0:T(4,128)} %get-tuple-element.31.owner_ref, f32[32,8,512]{2,1,0:T(8,128)} %get-tuple-element.32.grad_ref, f32[2,512,512]{2,1,0:T(8,128)} %get-tuple-element.33.left_ref, ...), custom_call_target="tpu_custom_call" | custom-call | flops 6442450944 | bytes 4718592 | tf_op jit(solution)/shard_map/cond/branch_1_fun/pallas_call | solution.py:325
  98.4 0.8 copy.16
  99.2 1.3 %copy.17 = f32[1,1,2,512,512]{4,3,2,1,0:T(8,128)} copy(f32[1,1,2,512,512]{4,3,2,1,0:T(8,128)S(1)} %bitcast.4) | data formatting | bytes 4194304
  100.6 1.3 %copy.18 = f32[1,1,2,512,512]{4,3,2,1,0:T(8,128)} copy(f32[1,1,2,512,512]{4,3,2,1,0:T(8,128)S(1)} %bitcast.5) | data formatting | bytes 4194304
  (2 shorter events, 0.0 us)

commit v3 on v2

v3 whole, which is shorter than its diff:
```python
import functools

import jax
import jax.numpy as jnp
from jax import lax
from jax.experimental import pallas as pl
from jax.experimental.pallas import tpu as pltpu
from jax.sharding import PartitionSpec as P

MESH = pl.DeviceIdType.MESH
F32 = jnp.float32
BF16 = jnp.bfloat16
I32 = jnp.int32
PLANE = 8
ROOMS = ((9, 3, 7), (12, 4, 8), (16, 8, 8))


def matmul(a, b):
    return jnp.dot(a, b, preferred_element_type=F32)


def total(x):
    return jnp.sum(x, keepdims=True)


def scaled_root(factor, eye):
    scaling = 2.5 * lax.rsqrt(total(factor * factor) + 1e-06)
    matrix = scaling * factor
    step_one = jnp.where(eye, 1.25, 0.0) - 0.25 * matrix
    step_one = step_one.astype(BF16)
    square = matmul(step_one, step_one).astype(BF16)
    fourth = matmul(square, square).astype(BF16)
    matrix = matmul(fourth, matrix.astype(BF16))
    step_two = (jnp.where(eye, 1.25, 0.0) - 0.25 * matrix).astype(BF16)
    return matmul(step_one, step_two), scaling


def square_iotas(n):
    return lax.broadcasted_iota(I32, (n, n), 0), lax.broadcasted_iota(I32, (n, n), 1)


def slots_of(owners):
    blocks = owners.shape[1]
    sub, lane = square_iotas(blocks)
    across = jnp.broadcast_to(owners, (blocks, blocks))
    owner = jnp.sum(jnp.where(sub == lane, across, 0), axis=1, keepdims=True)
    same = across == owner
    slot = jnp.sum(jnp.where(same & (lane < sub), 1, 0), axis=1, keepdims=True)
    slot_row = jnp.sum(jnp.where(same & (sub < lane), 1, 0), axis=0, keepdims=True)
    return owner, slot, slot_row, across


def gauge(owner_ref, level_ref):
    blocks = owner_ref.shape[1]
    wide = lax.broadcasted_iota(I32, (blocks, 128), 1)
    most = jnp.zeros((1, 128), I32)
    seconds = jnp.zeros((1, 128), I32)
    firsts = jnp.zeros((1, 128), I32)
    for t in range(owner_ref.shape[0]):
        owner, slot, _, _ = slots_of(owner_ref[t:t + 1, :])
        here = owner // PLANE == wide
        most = jnp.maximum(most, jnp.sum(jnp.where(here, 1, 0), axis=0, keepdims=True))
        seconds = jnp.maximum(seconds, jnp.sum(jnp.where(here & (slot == 1), 1, 0), axis=0, keepdims=True))
        firsts = jnp.maximum(firsts, jnp.sum(jnp.where(here & (slot == 0), 1, 0), axis=0, keepdims=True))
    level = jnp.zeros((1, 128), I32)
    for k, (room, early, late) in enumerate(ROOMS[:-1]):
        level = jnp.maximum(level, jnp.where((most > room) | (seconds > early) | (firsts > late), k + 1, 0))
    level_ref[0] = jnp.max(level)


BUNDLED, RANK, EARLY, LATE, PICK = range(5)


def plan(owners, me, n_dp, room, early, late):
    blocks = owners.shape[1]
    owner, slot, slot_row, across = slots_of(owners)
    z, z_row = owner // PLANE, across // PLANE
    slot_row = jnp.broadcast_to(slot_row, (blocks, blocks))
    ahead = jnp.where((z_row == z) & (slot_row == slot) & (across < owner), 1, 0)
    ahead = jnp.sum(ahead, axis=1, keepdims=True)
    rank = ahead + jnp.sum(jnp.where((z_row == z) & (slot_row > slot), 1, 0), axis=1, keepdims=True)
    wide = lax.broadcasted_iota(I32, (blocks, 128), 1)
    block = lax.broadcasted_iota(I32, (blocks, 128), 0)

    def row(where, value):
        return jnp.sum(jnp.where(where == wide, value, 0), axis=0, keepdims=True)

    place = owner % PLANE
    rows = (
        row(z * room + rank, block),
        row(slot * n_dp + owner, jnp.minimum(rank, jnp.where(slot == 1, early, room) - 1)),
        row(jnp.where(slot == 1, z * early + ahead, -1), place),
        row(jnp.where(slot == 0, z * late + ahead, -1), place),
        row(block, z * (early + late) + jnp.where(slot == 1, ahead, early + ahead)),
    )
    owned = jnp.sum(jnp.where(owners == me, 1, 0), keepdims=True)
    return jnp.concatenate(rows + rows[:3], axis=0), owned


def kernel(n_dp, n_tensor, room, early, late, depth, *refs):
    (owner_ref, grad_ref, left_ref, right_ref, step_ref, new_left_ref, new_right_ref,
     grads, packed, arrived, left, right, steps, returned, z_out, z_back,
     sums_z, sums_p, sums_y, mine_z, mine_p, mine_y, rows_v, rows_s,
     local_sem, state_sem, out_sem, z_send, z_recv, spread_send, spread_recv,
     part_send, part_recv, back_send, back_recv, sum_send, sum_recv) = refs[:-4 * depth]
    lists = refs[-4 * depth:]
    z_first, z_rest, x_second, x_first = (lists[k * depth:(k + 1) * depth] for k in range(4))
    me = lax.axis_index("dp")
    tensor = lax.axis_index("tensor")
    blocks, rows, order = grads.shape
    slots = arrived.shape[0]
    my_z = me // PLANE
    my_p = lax.rem(me, PLANE)
    offsets = [(k + 1) // 2 if k % 2 else (depth - k // 2) % depth for k in range(depth)]

    get_grads = pltpu.make_async_copy(grad_ref, grads, local_sem.at[0])
    get_grads.start()

    barrier = pltpu.get_barrier_semaphore()

    def greet(i, _):
        pl.semaphore_signal(barrier, inc=1, device_id=(my_z * PLANE + lax.rem(my_p + i, PLANE), tensor), device_id_type=MESH)
        return 0

    def greet_z(i, _):
        pl.semaphore_signal(barrier, inc=1, device_id=(lax.rem(my_z + i, depth) * PLANE + my_p, tensor), device_id_type=MESH)
        return 0

    lax.fori_loop(1, PLANE, greet, 0)
    lax.fori_loop(1, depth, greet_z, 0)
    for i in range(1, n_tensor):
        pl.semaphore_signal(barrier, inc=1, device_id=(me, lax.rem(tensor + i, n_tensor)), device_id_type=MESH)

    table, owned = plan(owner_ref[pl.ds(tensor, 1), :], me, n_dp, room, early, late)
    rows_v[...] = table
    put_rows = pltpu.make_async_copy(rows_v, rows_s, local_sem.at[1])
    put_rows.start()
    for slot in range(slots):
        pltpu.make_async_copy(left_ref.at[slot], left.at[slot], state_sem.at[0, slot]).start()
        pltpu.make_async_copy(right_ref.at[slot], right.at[slot], state_sem.at[1, slot]).start()

    get_grads.wait()
    tile = jnp.zeros((8, 128), F32)
    for k in range(order // 128):
        part = grads[:, :, k * 128:(k + 1) * 128]
        tile = tile + jnp.sum(part * part, axis=0)
    mine_z[...] = tile
    sums_z[my_z] = tile
    put_rows.wait()

    def pack(z, _):
        for q in range(room):
            z_out[z, q] = grads[rows_s[BUNDLED, z * room + q]]
        return 0

    lax.fori_loop(0, depth, pack, 0)
    z_first[0][...] = z_out[my_z, :early]
    z_rest[0][...] = z_out[my_z, early:]
    pl.semaphore_wait(barrier, PLANE + depth + n_tensor - 3)

    def copy(src, dst, send, recv, to):
        pltpu.make_async_remote_copy(
            src_ref=src, dst_ref=dst, send_sem=send, recv_sem=recv, device_id=to, device_id_type=MESH
        ).start()

    def wait(ref, sem):
        pltpu.make_async_copy(ref, ref, sem).wait()

    def along_z(i):
        return lax.rem(my_z + i, depth)

    def column(z):
        return (z * PLANE + my_p, tensor)

    def plane(i):
        p = lax.rem(my_p + i, PLANE)
        return p, (my_z * PLANE + p, tensor)

    def heard(sums, stage, count):
        wait(sums.at[pl.ds(0, count)], sum_recv.at[stage])
        wait(sums.at[pl.ds(0, count)], sum_send.at[stage])
        return jnp.sum(sums[...], axis=0)

    for i in offsets[1:]:
        z = along_z(i)
        copy(mine_z, sums_z.at[my_z], sum_send.at[0], sum_recv.at[0], column(z))
        copy(z_out.at[z, pl.ds(0, early)], z_first[i], z_send.at[1, i], z_recv.at[1, i], column(z))
    for i in offsets[1:]:
        z = along_z(i)
        copy(z_out.at[z, pl.ds(early, room - early)], z_rest[i], z_send.at[0, i], z_recv.at[0, i], column(z))

    def spread(slot, i):
        z = lax.rem(my_z + depth - i, depth)
        if i:
            wait(z_first[i] if slot else z_rest[i], z_recv.at[slot, i])

        def one(p, _):
            rank = rows_s[RANK, slot * n_dp + my_z * PLANE + p]
            if slot:
                packed[slot, p, z] = z_first[i][rank]
            else:
                before = z_first[i][jnp.minimum(rank, early - 1)]
                after = z_rest[i][jnp.maximum(rank - early, 0)]
                packed[slot, p, z] = jnp.where(rank < early, before, after)
            return 0

        lax.fori_loop(0, PLANE, one, 0)
        for k in range(1, PLANE):
            p, to = plane(k)
            copy(packed.at[slot, p, z], arrived.at[slot, z, my_p], spread_send.at[slot], spread_recv.at[slot], to)
        arrived[slot, z, my_p] = packed[slot, my_p, z]

    for i in offsets:
        spread(1, i)
    tile = heard(sums_z, 0, depth - 1)
    mine_p[...] = tile
    sums_p[my_p] = tile
    for i in range(1, PLANE):
        copy(mine_p, sums_p.at[my_p], sum_send.at[1], sum_recv.at[1], plane(i)[1])
    for i in offsets[:3]:
        spread(0, i)
    tile = heard(sums_p, 1, PLANE - 1)
    mine_y[...] = tile
    sums_y[tensor] = tile
    for i in range(1, n_tensor):
        copy(mine_y, sums_y.at[tensor], sum_send.at[2], sum_recv.at[2], (me, lax.rem(tensor + i, n_tensor)))
    for i in offsets[3:5]:
        spread(0, i)
    tile = heard(sums_y, 2, n_tensor - 1)
    clip = lax.rsqrt(total(tile) / (blocks * n_tensor * order * order) + 1e-06)
    clip_sq = clip * clip
    sub, lane = square_iotas(order)
    eye = sub == lane

    def update(slot):
        filled = jnp.where(owned > slot, 1.0, 0.0)
        wait(packed.at[slot, pl.ds(0, PLANE - 1)], spread_recv.at[slot])
        wait(left.at[slot], state_sem.at[0, slot])
        wait(right.at[slot], state_sem.at[1, slot])
        grad = arrived[slot].reshape(order, order)
        grad_sq = total(grad * grad)
        grad = grad.astype(BF16)
        gram = clip_sq * (0.1 / order)
        left_new = 0.9 * left[slot] + gram * lax.dot_general(
            grad, grad, (((1,), (1,)), ((), ())), preferred_element_type=F32)
        left[slot] = filled * left_new
        right_new = 0.9 * right[slot] + gram * lax.dot_general(
            grad, grad, (((0,), (0,)), ((), ())), preferred_element_type=F32)
        right[slot] = filled * right_new
        pltpu.make_async_copy(left.at[slot], new_left_ref.at[slot], out_sem.at[0, slot]).start()
        pltpu.make_async_copy(right.at[slot], new_right_ref.at[slot], out_sem.at[1, slot]).start()
        left_root, left_scale = scaled_root(left_new, eye)
        right_root, right_scale = scaled_root(right_new, eye)
        middle = matmul(left_root.astype(BF16), grad).astype(BF16)
        direction = matmul(middle, right_root.astype(BF16))
        scale = clip * jnp.sqrt(jnp.sqrt(left_scale * right_scale))
        ratio = jnp.sqrt(clip_sq * grad_sq + 1e-06) * lax.rsqrt(scale * scale * total(direction * direction) + 1e-06)
        steps[slot] = ((-ratio * scale) * direction).reshape(depth, PLANE, rows, order)

    def collect(slot):
        part = x_second if slot else x_first
        for i in offsets[::-1]:
            z = along_z(i)
            for k in range(1, PLANE):
                p, to = plane(k)
                copy(steps.at[slot, z, p], part[i].at[my_p], part_send.at[slot, i], part_recv.at[slot, i], to)
            part[i][my_p] = steps[slot, z, my_p]

    def send_back(slot, i):
        part = (x_second if slot else x_first)[i]
        start, size = (0, early) if slot else (early, late)
        z = along_z(i)
        wait(part.at[pl.ds(0, PLANE - 1)], part_recv.at[slot, i])

        def gather(q, _):
            z_back[z, start + q] = part[rows_s[EARLY if slot else LATE, my_z * size + q]]
            return 0

        lax.fori_loop(0, size, gather, 0)
        if i:
            copy(z_back.at[z, pl.ds(start, size)], returned.at[my_z, pl.ds(start, size)],
                 back_send.at[slot], back_recv.at[slot], column(z))

    update(1)
    for i in offsets[5:]:
        spread(0, i)
    collect(1)
    update(0)
    collect(0)
    for slot in (1, 0):
        for i in offsets[::-1]:
            send_back(slot, i)
    returned[my_z] = z_back[my_z]

    for slot in range(slots):
        pltpu.make_async_copy(left.at[slot], new_left_ref.at[slot], out_sem.at[0, slot]).wait()
        pltpu.make_async_copy(right.at[slot], new_right_ref.at[slot], out_sem.at[1, slot]).wait()
        wait(packed.at[slot, pl.ds(0, PLANE - 1)], spread_send.at[slot])
        for i in range(1, depth):
            wait(z_first[i] if slot else z_rest[i], z_send.at[slot, i])
        for i in range(depth):
            wait(x_first[i].at[pl.ds(0, PLANE - 1)], part_send.at[slot, i])
    for slot, size in ((1, early), (0, late)):
        seven = z_back.at[pl.ds(0, depth - 1), pl.ds(0, size)]
        wait(seven, back_send.at[slot])
        wait(seven, back_recv.at[slot])

    def pick(j, _):
        key = rows_s[PICK, j]
        step_ref[j] = returned[key // (early + late), lax.rem(key, early + late)]
        return 0

    lax.fori_loop(0, blocks, pick, 0)


def owner_step(n_dp, n_tensor, level, owner_map, grads, left_old, right_old):
    room, early, late = ROOMS[level]
    blocks, rows, order = grads.shape
    slots = left_old.shape[0]
    depth = n_dp // PLANE
    vmem = pl.BlockSpec(memory_space=pltpu.VMEM)
    hbm = pl.BlockSpec(memory_space=pl.ANY)
    dma = pltpu.SemaphoreType.DMA

    def pieces(*lead):
        return pltpu.VMEM(lead + (rows, order), F32)

    def tiles(*lead):
        return pltpu.VMEM(lead + (8, 128), F32)

    state = pltpu.VMEM((slots, order, order), F32)
    return pl.pallas_call(
        functools.partial(kernel, n_dp, n_tensor, room, early, late, depth),
        out_shape=(
            jax.ShapeDtypeStruct((blocks, rows, order), F32),
            jax.ShapeDtypeStruct((slots, order, order), F32),
            jax.ShapeDtypeStruct((slots, order, order), F32),
        ),
        in_specs=[vmem, hbm, hbm, hbm],
        out_specs=(vmem, hbm, hbm),
        scratch_shapes=[
            pieces(blocks), pieces(slots, PLANE, depth), pieces(slots, depth, PLANE), state, state,
            pieces(slots, depth, PLANE), pieces(depth, early + late), pieces(depth, room), pieces(depth, early + late),
            tiles(depth), tiles(PLANE), tiles(n_tensor), tiles(), tiles(), tiles(),
            pltpu.VMEM((8, 128), I32), pltpu.SMEM((8, 128), I32),
            dma((2,)), dma((2, slots)), dma((2, slots)), dma((slots, depth)), dma((slots, depth)),
            dma((slots,)), dma((slots,)), dma((slots, depth)), dma((slots, depth)), dma((slots,)), dma((slots,)),
            dma((3,)), dma((3,)),
        ] + [pieces(early)] * depth + [pieces(room - early)] * depth + [pieces(PLANE)] * (2 * depth),
        compiler_params=pltpu.CompilerParams(
            collective_id=level, has_side_effects=True, vmem_limit_bytes=48 * 2**20
        ),
        cost_estimate=pl.CostEstimate(
            flops=slots * 24 * order**3, bytes_accessed=18 * order * order, transcendentals=0),
    )(owner_map, grads, left_old, right_old)


def local(grad_blocks, owner_map, left_state, right_state):
    n_dp = lax.axis_size("dp")
    n_tensor = lax.axis_size("tensor")
    level = pl.pallas_call(
        gauge,
        out_shape=jax.ShapeDtypeStruct((1,), I32),
        in_specs=[pl.BlockSpec(memory_space=pltpu.VMEM)],
        out_specs=pl.BlockSpec(memory_space=pltpu.SMEM),
    )(owner_map)
    step_blocks, new_left, new_right = lax.switch(
        level[0],
        [functools.partial(owner_step, n_dp, n_tensor, k) for k in range(len(ROOMS))],
        owner_map, grad_blocks, left_state[0, 0], right_state[0, 0],
    )
    return (step_blocks, new_left[None, None], new_right[None, None])


def solution(mesh):
    state = P("tensor", "dp", None, None, None)
    return jax.shard_map(
        local,
        mesh=mesh,
        in_specs=(P("tensor", "dp", None), P(), state, state),
        out_specs=(P("tensor", "dp", None), state, state),
        check_vma=False,
    )
```

time: 102 us -> 90.2 us (0.88)
  the two profiles are of different devices: /device:TPU:16 before, /device:TPU:1 now
where the time goes in v3:
time: 90.2 us; the launch traced here: 90.1 us
  Pallas kernels  85.1 us (94%)
  local copies, waits for them, and re-layouts  3.43 us (4%)
  between operations  1.3 us (1%)
    pallas_call x1, Pallas kernels, owner_step(): pl.pallas_call(functools.partial(kernel, n_dp, n_tensor, room, early, lat...  83.5 us
    unnamed x3, local copies, waits for them, and re-layouts  3.43 us

profile of v3, /device:TPU:1, one launch (start us, length us, event | category | flops | bytes accessed | tf_op | source)
XLA Modules:
  0.0 90.1 jit_solution(2891089356784628884)
XLA Ops:
  0.6 1.6 %shard_map.67 = s32[1]{0:T(128)} custom-call(s32[4,32]{1,0:T(4,128)} %owner_ref.1), custom_call_target="tpu_custom_call" | custom-call | tf_op jit(solution)/shard_map/pallas_call | solution.py:361
  2.9 83.8 %conditional.1 = ((f32[32,8,512]{2,1,0:T(8,128)S(1)}, f32[2,512,512]{2,1,0:T(8,128)S(1)}, f32[2,512,512]{2,1,0:T(8,128)S(1)})) conditional(s32[]{:T(128)} %bitcast, (s32[4,32]{1,0:T(4,128)}, f32[32,8,512]{2,1,0:T(8,128)}, f32[2,512,512]{2,1,0:T(8,128)}, f32[2,512,512]{2,1,0:T(8,128)}) %tuple.41, (s32[4,32]{1,0:T(4,128)}, ...), branch_computations={%region_0.0_spmd, %region_1.0_spmd, %region_2.0_spmd} | conditional | flops 6442450944 | bytes 4718600 | solution.py:367
  2.9 83.5 %branch_0_fun.1 = (f32[32,8,512]{2,1,0:T(8,128)S(1)}, f32[2,512,512]{2,1,0:T(8,128)S(1)}, f32[2,512,512]{2,1,0:T(8,128)S(1)}) custom-call(s32[4,32]{1,0:T(4,128)} %get-tuple-element.35.refs_0_, f32[32,8,512]{2,1,0:T(8,128)} %get-tuple-element.36.refs_1_, f32[2,512,512]{2,1,0:T(8,128)} %get-tuple-element.37.refs_2_, f32[2,512,512]{2,1,0:T(8,128)} %get-tuple-element.38.refs_3_), custom_call_target="tpu_custom_call" | custom-call | flops 6442450944 | bytes 4718592 | tf_op jit(solution)/shard_map/cond/branch_0_fun/pallas_call | solution.py:332
  86.7 0.8 copy.19
  87.5 1.3 %copy.20 = f32[1,1,2,512,512]{4,3,2,1,0:T(8,128)} copy(f32[1,1,2,512,512]{4,3,2,1,0:T(8,128)S(1)} %bitcast.5) | data formatting | bytes 4194304
  88.8 1.3 %copy.21 = f32[1,1,2,512,512]{4,3,2,1,0:T(8,128)} copy(f32[1,1,2,512,512]{4,3,2,1,0:T(8,128)S(1)} %bitcast.6) | data formatting | bytes 4194304
